TPU v7x, 1024 devices: a whole 4x4x32 slice. The times are simulated.
1024 devices in a mesh: dp: 16 (over x, z_hi, core), tensor: 64 (over z_lo, y).
Axes of the slice: x: 4, y: 4, z: 32 (z_hi: 2, z_lo: 16; z = z_hi * 16 + z_lo), core: 2. Of those that a mesh axis runs over, the one named last changes fastest.
Arguments:
- tokens: bfloat16 [2048, 2560], P(('dp', 'tensor')), may hold values from -6 to 6
- cotangent: bfloat16 [2048, 2560], P(('dp', 'tensor')), may hold values from -6 to 6
- gate_weight: bfloat16 [2560, 12800], P('dp', 'tensor'), may hold values from -0.125 to 0.125
- up_weight: bfloat16 [2560, 12800], P('dp', 'tensor'), may hold values from -0.125 to 0.125
- down_weight: bfloat16 [12800, 2560], P('tensor', 'dp'), may hold values from -0.0546875 to 0.0546875
Outputs:
- input_grad: bfloat16 [2048, 2560], P(('dp', 'tensor'))
- grad_gate: bfloat16 [2560, 12800], P('dp', 'tensor')
- grad_up: bfloat16 [2560, 12800], P('dp', 'tensor')
- grad_down: bfloat16 [12800, 2560], P('tensor', 'dp')
All inputs are finite; a program needn't handle non-finite values.
Results may differ from a plain program's by a relative error of at most 0.017.
Values may be sent and summed in bfloat16 or wider, within the bound.
A program may use at most 64 MiB of HBM per device.

v0:
```python
import jax
import jax.numpy as jnp
from jax import lax
from jax.sharding import PartitionSpec as P


def local(tokens, cotangent, gate_weight, up_weight, down_weight):
    n_groups = lax.axis_size("dp")
    units = gate_weight.shape[1]
    group_tok, group_cot = (
        lax.all_gather(tokens, "tensor", axis=0, tiled=True),
        lax.all_gather(cotangent, "tensor", axis=0, tiled=True),
    )
    gate_full, up_full, down_full = (
        lax.all_gather(gate_weight, "dp", axis=0, tiled=True),
        lax.all_gather(up_weight, "dp", axis=0, tiled=True),
        lax.all_gather(down_weight, "dp", axis=1, tiled=True),
    )
    gate = jnp.dot(group_tok, gate_full, preferred_element_type=jnp.float32)
    up = jnp.dot(group_tok, up_full, preferred_element_type=jnp.float32)
    sig = jax.nn.sigmoid(gate)
    hidden = (gate * sig * up).astype(jnp.bfloat16)
    hidden_grad = jnp.einsum("td,fd->tf", group_cot, down_full, preferred_element_type=jnp.float32)
    up_grad = (hidden_grad * gate * sig).astype(jnp.bfloat16)
    gate_grad = (hidden_grad * up * sig * (1.0 + gate * (1.0 - sig))).astype(jnp.bfloat16)
    total = jnp.einsum("tf,df->td", gate_grad, gate_full, preferred_element_type=jnp.float32)
    input_grad = lax.psum_scatter(
        total + jnp.einsum("tf,df->td", up_grad, up_full, preferred_element_type=jnp.float32),
        "tensor",
        scatter_dimension=0,
        tiled=True,
    ).astype(jnp.bfloat16)
    part_gate = jnp.einsum("td,tf->df", group_tok, gate_grad, preferred_element_type=jnp.float32)
    part_up = jnp.einsum("td,tf->df", group_tok, up_grad, preferred_element_type=jnp.float32)
    part_down = jnp.einsum("td,tf->df", group_cot, hidden, preferred_element_type=jnp.float32)
    summed = (
        lax.psum_scatter(
            jnp.concatenate([part_gate, part_up, part_down], axis=1).astype(jnp.bfloat16),
            "dp",
            scatter_dimension=0,
            tiled=True,
        ).astype(jnp.float32)
        / n_groups
    )
    grad_gate = summed[:, :units].astype(jnp.bfloat16)
    grad_up = summed[:, units : 2 * units].astype(jnp.bfloat16)
    grad_down = summed[:, 2 * units :].T.astype(jnp.bfloat16)
    return (input_grad, grad_gate, grad_up, grad_down)


def solution(mesh):
    placed = (
        P(("dp", "tensor"), None),
        P(("dp", "tensor"), None),
        P("dp", "tensor"),
        P("dp", "tensor"),
        P("tensor", "dp"),
    )
    return jax.shard_map(
        local,
        mesh=mesh,
        in_specs=placed,
        out_specs=(
            P(("dp", "tensor"), None),
            P("dp", "tensor"),
            P("dp", "tensor"),
            P("tensor", "dp"),
        ),
        check_vma=False,
    )
```

profile of v0, /device:TPU:6, one launch (start us, length us, event | category | flops | bytes accessed | tf_op | source)
XLA Modules:
  0.0 1905.9 jit_solution(17330169498363768651)
XLA Ops:
  7.2 0.0 reduce-scatter.4.cloned.1.call-start
  7.2 426.0 %all-gather.1 = bf16[64,2,2560]{2,1,0:T(2,128)(2,1)S(1)} all-gather(bf16[1,2,2560]{2,1,0:T(2,128)(2,1)} %bitcast.27), channel_id=1, replica_groups=mesh['dp'=16,'tensor'=64] {'tensor'}, dimensions={0}, use_global_device_ids=true | all-gather | bytes 665600 | tf_op jit(solution)/shard_map/all_gather | solution.py:11
  433.2 0.2 reshape.11
  433.5 95.6 %all_gather.19 = bf16[2560,200]{1,0:T(8,128)(2,1)S(1)} all-gather(bf16[160,200]{1,0:T(8,128)(2,1)S(1)} %copy-done.4), channel_id=1, replica_groups=mesh['dp'=16,'tensor'=64] {'dp'}, dimensions={0}, use_global_device_ids=true | all-gather | bytes 1088000 | tf_op jit(solution)/shard_map/all_gather | solution.py:15
  529.1 82.9 %all_gather.18 = bf16[2560,200]{1,0:T(8,128)(2,1)S(1)} all-gather(bf16[160,200]{1,0:T(8,128)(2,1)S(1)} %copy-done.5), channel_id=1, replica_groups=mesh['dp'=16,'tensor'=64] {'dp'}, dimensions={0}, use_global_device_ids=true | all-gather | bytes 1088000 | tf_op jit(solution)/shard_map/all_gather | solution.py:16
  612.0 0.6 fusion.6
  612.6 0.0 copy-start.7
  612.7 0.6 fusion.5
  613.3 0.0 copy-start.6
  613.3 0.1 copy-done.7
  613.4 388.5 %all-gather = bf16[64,2,2560]{2,1,0:T(2,128)(2,1)S(1)} all-gather(bf16[1,2,2560]{2,1,0:T(2,128)(2,1)S(1)} %bitcast.28), channel_id=1, replica_groups=mesh['dp'=16,'tensor'=64] {'tensor'}, dimensions={0}, use_global_device_ids=true | all-gather | bytes 665600 | tf_op jit(solution)/shard_map/all_gather | solution.py:12
  1001.9 0.2 reshape.9
  1002.1 77.5 %all_gather.16 = bf16[200,2560]{0,1:T(8,128)(2,1)S(1)} all-gather(bf16[200,160]{0,1:T(8,128)(2,1)S(1)} %copy-done.6), channel_id=1, replica_groups=mesh['dp'=16,'tensor'=64] {'dp'}, dimensions={1}, use_global_device_ids=true | all-gather | bytes 1088000 | tf_op jit(solution)/shard_map/all_gather | solution.py:17
  1079.6 0.4 fusion.2
  1080.0 0.6 multiply_convert_fusion.2
  1080.6 0.4 fusion.1
  1081.0 0.4 fusion
  1081.5 0.2 pad_maximum_fusion
  1081.7 3.4 copy.15
  1085.1 0.0 reduce-scatter.4.cloned.1.call-update
  1085.1 1.3 copy-done.3
  1086.4 0.6 fusion.7
  1087.0 0.7 copy-done.1
  1087.7 0.6 convolution_add_fusion
  1088.3 1.3 dynamic-slice
  1090.3 804.7 %all-reduce.2 = bf16[128,2560]{1,0:T(8,128)(2,1)S(1)} all-reduce(f32[128,2560]{1,0:T(8,128)S(1)} %convolution_add_fusion), channel_id=2, replica_groups=mesh['dp'=16,'tensor'=64] {'tensor'}, use_global_device_ids=true, to_apply=%region_0.0.clone | all-reduce | flops 327680 | bytes 1966080
  1895.0 0.6 dynamic-slice_convert_fusion
  1895.6 1.1 copy.16
  1896.7 0.1 multiply_convert_fusion
  1896.8 0.7 copy.12
  1897.5 0.7 copy.13
  1898.3 0.7 copy.14
  (13 shorter events, 0.0 us)
Async XLA Ops:
  7.2 426.3 %copy-start.4 = (bf16[160,200]{1,0:T(8,128)(2,1)S(1)}, bf16[160,200]{1,0:T(8,128)(2,1)}, u32[]{:S(2)}) copy-start(bf16[160,200]{1,0:T(8,128)(2,1)} %param.7) | copy-start | bytes 192004
  7.2 1888.4 %reduce-scatter.4.cloned.1.call-start = ((), (), s32[]{:S(2)}) async-start(), calls=%async_computation.1 | async-start | bytes 3481600
  433.2 95.9 %copy-start.5 = (bf16[160,200]{1,0:T(8,128)(2,1)S(1)}, bf16[160,200]{1,0:T(8,128)(2,1)}, u32[]{:S(2)}) copy-start(bf16[160,200]{1,0:T(8,128)(2,1)} %param.8) | copy-start | bytes 192004
  529.1 83.5 %copy-start.2 = (bf16[2560,200]{1,0:T(8,128)(2,1)}, bf16[2560,200]{1,0:T(8,128)(2,1)S(1)}, u32[]{:S(2)}) copy-start(bf16[2560,200]{1,0:T(8,128)(2,1)S(1)} %all_gather.19) | copy-start | bytes 3072004
  612.0 1.2 copy-start
  612.6 0.7 copy-start.7
  613.3 388.9 %copy-start.6 = (bf16[200,160]{0,1:T(8,128)(2,1)S(1)}, bf16[200,160]{0,1:T(8,128)(2,1)}, u32[]{:S(2)}) copy-start(bf16[200,160]{0,1:T(8,128)(2,1)} %param.9) | copy-start | bytes 192004
  1085.1 1.3 copy-start.3
  1086.4 1.3 copy-start.1
Sparse Core Ops, SparseCore 0:
  1085.3 214.5 reduce-scatter.3
where the time goes:
time: 1920 us; the launch traced here: 1910 us
  blocking collectives  1880 us (98%)
    unnamed x1, blocking collectives  805 us
    all_gather x1, blocking collectives, local(): lax.all_gather(tokens, 'tensor', axis=0, tiled=True)  426 us
    all_gather x1, blocking collectives, local(): lax.all_gather(cotangent, 'tensor', axis=0, tiled=True)  389 us
    all_gather x1, blocking collectives, local(): lax.all_gather(gate_weight, 'dp', axis=0, tiled=True)  95.6 us
    all_gather x1, blocking collectives, local(): lax.all_gather(up_weight, 'dp', axis=0, tiled=True)  82.9 us
    all_gather x1, blocking collectives, local(): lax.all_gather(down_weight, 'dp', axis=1, tiled=True)  77.5 us
  transfers between devices with their start and end apart: 1, of which 0 were waited for; matrix products, arithmetic and copies ran while one was open for 0% of the time, Pallas kernels for 0%

commit v1 on v0

v1 whole, which is shorter than its diff:
```python
import functools

import jax
import jax.numpy as jnp
from jax import lax
from jax.experimental import pallas as pl
from jax.experimental.pallas import tpu as pltpu
from jax.sharding import PartitionSpec as P

MESH = pl.DeviceIdType.MESH
BF = jnp.bfloat16
F32 = jnp.float32
SHARD = 80
GSH = 48
UNITS = 200
WIDTH = 640
ROWS = 160


def kernel(
    xp_ref, wp_ref, ig_ref, gr_ref,
    tokb, xf, xs, wbuf, fwd, ab, of, ob, pbuf, crecv, psum, xrecv, zsend, zrecv, acc,
    yrecv, ys, nrecv, ns, frecv, ssem, rsem,
):
    dp = lax.axis_index("dp")
    t = lax.axis_index("tensor")
    x, h, c = dp // 4, (dp // 2) % 2, dp % 2
    zl, y = t // 4, t % 4
    q, j = zl // 4, zl % 4

    def dev(x=x, h=h, c=c, q=q, j=j, y=y):
        return ((x * 2 + h) * 2 + c, (q * 4 + j) * 4 + y)

    def up4(v, k):
        return lax.rem(v + k, 4)

    far = [dev(q=up4(q, k)) for k in (1, 2, 3)]
    near = [dev(j=up4(j, k)) for k in (1, 2, 3)]
    ypeer = [dev(y=up4(y, k)) for k in (1, 2, 3)]
    xpeer = [dev(x=up4(x, k)) for k in (1, 2, 3)]
    zpeer = dev(h=1 - h)
    sib = dev(c=1 - c)
    partners = far + near + ypeer + xpeer + [zpeer, sib]

    counter = [0]
    started = []

    def send(src, dst, device):
        i = counter[0]
        counter[0] += 1
        cp = pltpu.make_async_remote_copy(
            src_ref=src, dst_ref=dst, send_sem=ssem.at[i], recv_sem=rsem.at[i],
            device_id=device, device_id_type=MESH,
        )
        cp.start()
        started.append(cp)
        return cp

    barrier = pltpu.get_barrier_semaphore()
    for d in partners:
        pl.semaphore_signal(barrier, inc=1, device_id=d, device_id_type=MESH)

    slot = y * 16 + j * 4 + q
    tokb[slot] = xp_ref[...]
    wbuf[dp] = wp_ref[...]
    of[...] = jnp.zeros_like(of)
    pl.semaphore_wait(barrier, len(partners))

    far_c = [send(tokb.at[slot], tokb.at[slot], far[k]) for k in range(3)]
    xown = [send(wbuf.at[dp], wbuf.at[dp], xpeer[k]) for k in range(3)]
    core_c = [send(wbuf.at[dp], wbuf.at[dp], sib)]
    halves = [pl.ds(0, 80), pl.ds(80, 80)]
    z_c = [send(wbuf.at[dp, r], wbuf.at[dp, r], zpeer) for r in halves]

    for k in range(3):
        xown[k].wait_recv()
        s = (up4(x, 3 - k) * 2 + h) * 2 + c
        core_c.append(send(wbuf.at[s], wbuf.at[s], sib))
    for cp in far_c:
        cp.wait_recv()
    chunk = pl.ds(y * 16 + j * 4, 4)
    near_c = [send(tokb.at[chunk], tokb.at[chunk], near[k]) for k in range(3)]
    for cp in near_c:
        cp.wait_recv()
    chunk = pl.ds(y * 16, 16)
    y_c = [send(tokb.at[chunk], tokb.at[chunk], ypeer[k]) for k in range(3)]

    other = (x * 2 + 1 - h) * 2 + c
    xfw = []
    for i, r in enumerate(halves):
        z_c[i].wait_recv()
        xfw.append([send(wbuf.at[other, r], wbuf.at[other, r], xpeer[k]) for k in range(3)])
        core_c.append(send(wbuf.at[other, r], wbuf.at[other, r], sib))
        if i == 0:
            for cp in y_c:
                cp.wait_recv()
            xf[...] = tokb[...].astype(F32).reshape(64 * SHARD, 128)
            for a in range(2):
                for k in range(2):
                    for b in range(20):
                        v = xf[pl.ds(a * 40 + k * 20 + b, 64, stride=SHARD), :]
                        xs[pl.ds(a * 128 + k * 64, 64), pl.ds(b * 128, 128)] = v.astype(BF)
    for i, r in enumerate(halves):
        for k in range(3):
            xfw[i][k].wait_recv()
            s = (up4(x, 3 - k) * 2 + 1 - h) * 2 + c
            core_c.append(send(wbuf.at[s, r], wbuf.at[s, r], sib))
    for cp in core_c:
        cp.wait_recv()

    fwd[...] = jnp.zeros_like(fwd)

    def forward(i, carry):
        d = pl.ds(pl.multiple_of(i * 640, 640), 640)
        w = wbuf[pl.ds(i * 4, 4)].reshape(640, WIDTH)
        fwd[...] += jnp.dot(xs[:, d], w, preferred_element_type=F32)
        return carry

    lax.fori_loop(0, 4, forward, 0)
    g = fwd[0:128, :]
    gate = g[:, :256]
    upv = pltpu.roll(g, WIDTH - UNITS, 1)[:, :256]
    hg = pltpu.roll(fwd[128:256, :], WIDTH - 2 * UNITS, 1)[:, :256]
    sig = 1.0 / (1.0 + jnp.exp(-gate))
    keep = lax.broadcasted_iota(jnp.int32, (128, 256), 1) < UNITS
    rest = jnp.zeros((128, WIDTH - 256), F32)

    def wide(v, shift):
        v = jnp.concatenate([jnp.where(keep, v, 0.0), rest], axis=1)
        return pltpu.roll(v, shift, 1) if shift else v

    hidden = wide(gate * sig * upv, 2 * UNITS)
    gg = wide(hg * upv * sig * (1.0 + gate * (1.0 - sig)), 0)
    ug = wide(hg * gate * sig, UNITS)
    ab[0:128, :] = (gg + ug).astype(BF)
    ab[128:256, :] = hidden.astype(BF)

    def partial(i, carry):
        d = pl.ds(pl.multiple_of(i * 640, 640), 640)
        p = lax.dot_general(xs[:, d], ab[...], (((0,), (0,)), ((), ())), preferred_element_type=F32)
        p = p.astype(BF)
        for b in range(4):
            pbuf[(b % 2) * 8 + (b // 2) * 4 + i] = p[b * ROWS : (b + 1) * ROWS, :]
        return carry

    lax.fori_loop(0, 4, partial, 0)
    pc = []
    for hh in (1 - h, h):
        src = pl.ds((1 - c) * 8 + hh * 4, 4)
        pc.append(send(pbuf.at[src], crecv.at[pl.ds(hh * 4, 4)], sib))

    for i in range(4):
        w = wbuf[i * 4 : i * 4 + 4].reshape(640, WIDTH)
        tot = lax.dot_general(ab[0:128, :], w, (((1,), (1,)), ((), ())), preferred_element_type=F32)
        for k in range(2):
            for b in range(5):
                of[pl.ds(k * 20 + i * 5 + b, 64, stride=GSH), :] = tot[
                    k * 64 : k * 64 + 64, b * 128 : b * 128 + 128
                ]
    ob[...] = of[...].reshape(64, GSH, 128).astype(BF)
    yg = [
        send(ob.at[pl.ds(up4(y, k + 1) * 16, 16)], yrecv.at[k], ypeer[k]) for k in range(3)
    ]

    px = []
    for n, hh in enumerate((1 - h, h)):
        pc[n].wait_recv()
        for i in range(4):
            a = pbuf[c * 8 + hh * 4 + i].astype(F32) + crecv[hh * 4 + i].astype(F32)
            psum[hh * 4 + i] = a.astype(BF)
        px.append(
            [send(psum.at[hh * 4 + up4(x, k + 1)], xrecv.at[n, k], xpeer[k]) for k in range(3)]
        )
    for n, hh in enumerate((1 - h, h)):
        for cp in px[n]:
            cp.wait_recv()
        a = psum[hh * 4 + x].astype(F32)
        for k in range(3):
            a = a + xrecv[n, k].astype(F32)
        if n == 0:
            zsend[...] = a.astype(BF)
            pz = send(zsend, zrecv, zpeer)
            for cp in yg:
                cp.wait_recv()
            s = ob[pl.ds(y * 16, 16)].astype(F32)
            for k in range(3):
                s = s + yrecv[k].astype(F32)
            ys[...] = s.astype(BF)
            ng = [
                send(ys.at[pl.ds(up4(j, k + 1) * 4, 4)], nrecv.at[k], near[k]) for k in range(3)
            ]
        else:
            acc[...] = a
    for cp in ng:
        cp.wait_recv()
    s = ys[pl.ds(j * 4, 4)].astype(F32)
    for k in range(3):
        s = s + nrecv[k].astype(F32)
    ns[...] = s.astype(BF)
    fg = [send(ns.at[up4(q, k + 1)], frecv.at[k], far[k]) for k in range(3)]
    for cp in fg:
        cp.wait_recv()
    s = ns[q].astype(F32)
    for k in range(3):
        s = s + frecv[k].astype(F32)
    ig_ref[...] = s.astype(BF)
    pz.wait_recv()
    gr_ref[...] = ((acc[...] + zrecv[...].astype(F32)) * (1.0 / 16.0)).astype(BF)
    for cp in started:
        cp.wait_send()


COPIES = 64


def local(tokens, cotangent, gate_weight, up_weight, down_weight):
    xp = jnp.concatenate([tokens, cotangent], axis=0).reshape(SHARD, 128)
    wp = jnp.concatenate(
        [gate_weight, up_weight, down_weight.T, jnp.zeros((ROWS, WIDTH - 3 * UNITS), BF)], axis=1
    )
    vmem = pl.BlockSpec(memory_space=pltpu.VMEM)
    ig, gr = pl.pallas_call(
        kernel,
        name="swiglu_backward",
        out_shape=(
            jax.ShapeDtypeStruct((GSH, 128), BF),
            jax.ShapeDtypeStruct((ROWS, WIDTH), BF),
        ),
        in_specs=[vmem, vmem],
        out_specs=(vmem, vmem),
        scratch_shapes=[
            pltpu.VMEM((64, SHARD, 128), BF),
            pltpu.VMEM((64 * SHARD, 128), F32),
            pltpu.VMEM((256, 2560), BF),
            pltpu.VMEM((16, ROWS, WIDTH), BF),
            pltpu.VMEM((256, WIDTH), F32),
            pltpu.VMEM((256, WIDTH), BF),
            pltpu.VMEM((64 * GSH, 128), F32),
            pltpu.VMEM((64, GSH, 128), BF),
            pltpu.VMEM((16, ROWS, WIDTH), BF),
            pltpu.VMEM((8, ROWS, WIDTH), BF),
            pltpu.VMEM((8, ROWS, WIDTH), BF),
            pltpu.VMEM((2, 3, ROWS, WIDTH), BF),
            pltpu.VMEM((ROWS, WIDTH), BF),
            pltpu.VMEM((ROWS, WIDTH), BF),
            pltpu.VMEM((ROWS, WIDTH), F32),
            pltpu.VMEM((3, 16, GSH, 128), BF),
            pltpu.VMEM((16, GSH, 128), BF),
            pltpu.VMEM((3, 4, GSH, 128), BF),
            pltpu.VMEM((4, GSH, 128), BF),
            pltpu.VMEM((3, GSH, 128), BF),
            pltpu.SemaphoreType.DMA((COPIES,)),
            pltpu.SemaphoreType.DMA((COPIES,)),
        ],
        compiler_params=pltpu.CompilerParams(
            collective_id=0, has_side_effects=True, vmem_limit_bytes=50 * 1024 * 1024
        ),
    )(xp, wp)
    input_grad = ig[:40].reshape(2, 2560)
    return (
        input_grad,
        gr[:, :UNITS],
        gr[:, UNITS : 2 * UNITS],
        gr[:, 2 * UNITS : 3 * UNITS].T,
    )


def solution(mesh):
    placed = (
        P(("dp", "tensor"), None),
        P(("dp", "tensor"), None),
        P("dp", "tensor"),
        P("dp", "tensor"),
        P("tensor", "dp"),
    )
    return jax.shard_map(
        local,
        mesh=mesh,
        in_specs=placed,
        out_specs=(
            P(("dp", "tensor"), None),
            P("dp", "tensor"),
            P("dp", "tensor"),
            P("tensor", "dp"),
        ),
        check_vma=False,
    )
```

time: 1920 us -> 174 us (0.09)
  blocking collectives: 1880 us -> 0 us
  Pallas kernels: 0 us -> 169 us
    all_gather x5 -> x0, blocking collectives: 1070 us -> none  [the longest x1 426 us: local(): lax.all_gather(tokens, 'tensor', axis=0, tiled=True)]
    unnamed x1 -> x0, blocking collectives: 805 us -> none
    pallas_call x0 -> x1, Pallas kernels: none -> 169 us  [local(): pl.pallas_call(kernel, name='swiglu_backward', out_shape=(jax.ShapeDtypeS...]
  transfers between devices with their start and end apart: 1 -> 0, of which waited for: 0 -> 0; matrix products, arithmetic and copies ran while one was open for 0% -> 0% of each run, Pallas kernels for 0% -> 0%
where the time goes in v1:
time: 174 us; the launch traced here: 173 us
  Pallas kernels  169 us (97%)
  other arithmetic  1.8 us (1%)
    pallas_call x1, Pallas kernels, local(): pl.pallas_call(kernel, name='swiglu_backward', out_shape=(jax.ShapeDtypeS...  169 us

profile of v1, /device:TPU:6, one launch (start us, length us, event | category | flops | bytes accessed | tf_op | source)
XLA Modules:
  0.0 173.2 jit_solution(14863649526548270440)
XLA Ops:
  0.6 0.0 copy-start
  0.7 0.1 pad.3.clone
  0.7 0.7 pad_maximum_fusion
  1.5 0.0 copy-done
  1.5 1.1 maximum_maximum_fusion.wp_ref
  2.6 169.2 %swiglu_backward.1 = (bf16[48,128]{1,0:T(8,128)(2,1)S(1)}, bf16[160,640]{1,0:T(8,128)(2,1)S(1)}) custom-call(bf16[80,128]{1,0:T(8,128)(2,1)S(1)} %reshape.14.xp_ref, bf16[160,640]{1,0:T(8,128)(2,1)S(1)} %maximum_maximum_fusion.wp_ref), custom_call_target="tpu_custom_call" | custom-call | tf_op jit(solution)/shard_map/swiglu_backward/pallas_call | solution.py:222
  171.8 0.6 reshape.15
  172.4 0.8 slice_bitcast_fusion
  (3 shorter events, 0.0 us)
Async XLA Ops:
  0.6 0.9 copy-start

commit v2 on v0

v2 whole, which is shorter than its diff:
```python
import jax
import jax.numpy as jnp
from jax import lax
from jax.experimental import pallas as pl
from jax.experimental.pallas import tpu as pltpu
from jax.sharding import PartitionSpec as P

MESH = pl.DeviceIdType.MESH
BF = jnp.bfloat16
F32 = jnp.float32
SHARD = 80
GROWS = 40
GPAD = 48
UNITS = 100
PACK = 320
WIDTH = 2 * PACK
HALF = 80
COPIES = 128


def kernel(
    xp_ref, wp_ref, ig_ref, gr_ref,
    tokb, xf, xs, wbuf, wz, fwd, ab1, ab2, of, ob, pbuf, crecv, psum, xrecv, zsum, pz,
    yrecv, ys, nrecv, n2recv, fs, rp, rm, sp, sm, ssem, rsem,
):
    dp = lax.axis_index("dp")
    t = lax.axis_index("tensor")
    x, h, c = dp // 4, (dp // 2) % 2, dp % 2
    zl, y = t // 4, t % 4
    z = h * 16 + zl
    q, j = z // 4, z % 4

    def dev(x=x, z=z, c=c, y=y):
        z = lax.rem(z + 32, 32)
        return ((x * 2 + z // 16) * 2 + c, lax.rem(z, 16) * 4 + y)

    def up4(v, k):
        return lax.rem(v + k, 4)

    zp4, zm4, zp1, zm1, zp2, zm2 = [dev(z=z + k) for k in (4, -4, 1, -1, 2, -2)]
    ypeer = [dev(y=up4(y, k)) for k in (1, 2, 3)]
    xpeer = [dev(x=up4(x, k)) for k in (1, 2, 3)]
    sib = dev(c=1 - c)
    partners = [zp4, zm4, zp1, zm1, zp2, zm2] + ypeer + xpeer + [sib]
    turn = 4 - 8 * c
    ahead, behind = dev(z=z + turn), dev(z=z - turn)
    parts = [(ahead, turn, 0), (ahead, turn, 16), (ahead, turn, 32), (behind, -turn, 48), (behind, -turn, 64)]

    counter = [0]
    started = []

    def send(src, dst, device):
        i = counter[0]
        counter[0] += 1
        cp = pltpu.make_async_remote_copy(
            src_ref=src, dst_ref=dst, send_sem=ssem.at[i], recv_sem=rsem.at[i],
            device_id=device, device_id_type=MESH,
        )
        cp.start()
        started.append(cp)
        return cp

    barrier = pltpu.get_barrier_semaphore()
    for d in partners:
        pl.semaphore_signal(barrier, inc=1, device_id=d, device_id_type=MESH)
    base = y * 32 + j * 8

    def at(k):
        return base + lax.rem(q + k + 8, 8)

    tokb[at(0)] = xp_ref[...]
    wbuf[dp] = wp_ref[h]
    fs[...] = jnp.zeros_like(fs)
    pl.semaphore_wait(barrier, len(partners))

    fa = send(tokb.at[at(0)], tokb.at[at(0)], zp4)
    fb = send(tokb.at[at(0)], tokb.at[at(0)], zm4)
    zw = [
        send(wp_ref.at[1 - h, pl.ds(r, 16)], wz.at[0, pl.ds(r, 16)], d) for d, s, r in parts
    ]
    xown = [send(wbuf.at[dp], wbuf.at[dp], xpeer[k]) for k in range(3)]
    core_c = [send(wbuf.at[dp], wbuf.at[dp], sib)]

    def relay(step):
        for i, (d, s, r) in enumerate(parts):
            zw[i].wait_recv()
            rows = pl.ds(r, 16)
            if step < 3:
                dst = wz.at[step, rows]
            else:
                to = lax.rem(z + s + 32, 32) // 16
                dst = wbuf.at[(x * 2 + 1 - to) * 2 + c, rows]
            zw[i] = send(wz.at[step - 1, rows], dst, d)

    for step in (1, 2):
        fa.wait_recv()
        fa = send(tokb.at[at(-step)], tokb.at[at(-step)], zp4)
        fb.wait_recv()
        fb = send(tokb.at[at(step)], tokb.at[at(step)], zm4)
        relay(step)
        if step == 1:
            for k in range(3):
                xown[k].wait_recv()
                s = (up4(x, 3 - k) * 2 + h) * 2 + c
                core_c.append(send(wbuf.at[s], wbuf.at[s], sib))
    fa.wait_recv()
    fa = send(tokb.at[at(-3), pl.ds(0, 48)], tokb.at[at(-3), pl.ds(0, 48)], zp4)
    fb.wait_recv()
    fb = send(tokb.at[at(3), pl.ds(48, 32)], tokb.at[at(3), pl.ds(48, 32)], zm4)
    relay(3)
    fa.wait_recv()
    fb.wait_recv()

    def ysend(residue):
        piece = pl.ds(y * 32 + residue * 8, 8)
        return [send(tokb.at[piece], tokb.at[piece], ypeer[k]) for k in range(3)]

    mine = pl.ds(base, 8)
    low, high = pl.ds(base, 4), pl.ds(base + 4, 4)
    n1 = [send(tokb.at[mine], tokb.at[mine], d) for d in (zp1, zm1)]
    n2 = [send(tokb.at[low], tokb.at[low], zp2), send(tokb.at[high], tokb.at[high], zm2)]
    yc = [ysend(j)]
    n1[0].wait_recv()
    yc.append(ysend(up4(j, 3)))
    n1[1].wait_recv()
    yc.append(ysend(up4(j, 1)))
    for cp in n2:
        cp.wait_recv()
    yc.append(ysend(up4(j, 2)))

    other = (x * 2 + 1 - h) * 2 + c
    for cp in zw:
        cp.wait_recv()
    xfw = [send(wbuf.at[other], wbuf.at[other], xpeer[k]) for k in range(3)]
    core_c.append(send(wbuf.at[other], wbuf.at[other], sib))

    def unpack(yy):
        xf[...] = tokb[pl.ds(yy * 32, 32)].astype(F32).reshape(32 * SHARD, 128)
        for a in range(2):
            for k in range(2):
                rows = pl.ds(pl.multiple_of(a * 256 + k * 128 + yy * 32, 32), 32)
                for b in range(20):
                    v = xf[pl.ds(a * 40 + k * 20 + b, 32, stride=SHARD), :]
                    xs[rows, pl.ds(b * 128, 128)] = v.astype(BF)

    unpack(y)
    for k in range(3):
        xfw[k].wait_recv()
        s = (up4(x, 3 - k) * 2 + 1 - h) * 2 + c
        core_c.append(send(wbuf.at[s], wbuf.at[s], sib))
    for k in (0, 2, 1):
        for piece in yc:
            piece[k].wait_recv()
        unpack(up4(y, 3 - k))
    for cp in core_c:
        cp.wait_recv()

    w = wbuf[...].reshape(1280, WIDTH)
    fwd[...] = jnp.dot(xs[:, 1280:2560], w, preferred_element_type=F32)
    fwd[...] = jnp.dot(xs[:, 0:1280], w, preferred_element_type=F32) + pltpu.roll(
        fwd[...], PACK, 1
    )
    g = fwd[0:256, :256]
    gate = g[:, :128]
    upv = pltpu.roll(g, 256 - UNITS, 1)[:, :128]
    hg = pltpu.roll(fwd[256:512, :384], 384 - 2 * UNITS, 1)[:, :128]
    sig = 1.0 / (1.0 + jnp.exp(-gate))
    keep = lax.broadcasted_iota(jnp.int32, (256, 128), 1) < UNITS
    rest = jnp.zeros((256, WIDTH - 128), F32)

    def wide(v):
        return jnp.concatenate([jnp.where(keep, v, 0.0), rest], axis=1)

    gg = wide(hg * upv * sig * (1.0 + gate * (1.0 - sig)))
    a = gg + pltpu.roll(wide(hg * gate * sig), UNITS, 1)
    ab1[0:256, :] = a.astype(BF)
    ab2[0:256, :] = pltpu.roll(a, PACK, 1).astype(BF)
    a = wide(gate * sig * upv)
    ab1[256:512, :] = pltpu.roll(a, 2 * UNITS, 1).astype(BF)
    ab2[256:512, :] = pltpu.roll(a, PACK + 2 * UNITS, 1).astype(BF)

    tr = (((0,), (0,)), ((), ()))
    for i in range(2):
        p = lax.dot_general(
            xs[:, i * 640 : i * 640 + 640], ab1[...], tr, preferred_element_type=F32
        ) + lax.dot_general(
            xs[:, 1280 + i * 640 : 1920 + i * 640], ab2[...], tr, preferred_element_type=F32
        )
        p = p.astype(BF)
        for b in range(8):
            pbuf[(b % 2) * 8 + ((b // 2) % 2) * 4 + i * 2 + b // 4] = p[b * HALF : (b + 1) * HALF, :]
    pc = []
    for hh in (1 - h, h):
        src = pl.ds((1 - c) * 8 + hh * 4, 4)
        pc.append(send(pbuf.at[src], crecv.at[pl.ds(hh * 4, 4)], sib))

    nt = (((1,), (1,)), ((), ()))
    for e, ab in enumerate((ab1, ab2)):
        for i in range(2):
            w = wbuf[i * 8 : i * 8 + 8].reshape(640, WIDTH)
            tot = lax.dot_general(ab[0:256, :], w, nt, preferred_element_type=F32)
            for k in range(2):
                for b in range(5):
                    of[pl.ds(k * 20 + e * 10 + i * 5 + b, 128, stride=GROWS), :] = tot[
                        k * 128 : k * 128 + 128, b * 128 : b * 128 + 128
                    ]
    ob[...] = of[...].reshape(64, 80, 128).astype(BF)
    yg = [
        send(ob.at[pl.ds(up4(y, k + 1) * 16, 16)], yrecv.at[k], ypeer[k]) for k in range(3)
    ]

    px = []
    for n, hh in enumerate((1 - h, h)):
        pc[n].wait_recv()
        for i in range(4):
            a = pbuf[c * 8 + hh * 4 + i].astype(F32) + crecv[hh * 4 + i].astype(F32)
            psum[hh * 4 + i] = a.astype(BF)
        px.append(
            [send(psum.at[hh * 4 + up4(x, k + 1)], xrecv.at[n, k], xpeer[k]) for k in range(3)]
        )

    def xsum(n, hh):
        for cp in px[n]:
            cp.wait_recv()
        a = psum[hh * 4 + x].astype(F32)
        for k in range(3):
            a = a + xrecv[n, k].astype(F32)
        return (a * (1.0 / 16.0)).astype(BF)

    zsum[...] = xsum(0, 1 - h)
    zw = [send(zsum.at[pl.ds(r, 16)], pz.at[0, pl.ds(r, 16)], d) for d, s, r in parts]

    for cp in yg:
        cp.wait_recv()
    a = ob[pl.ds(y * 16, 16)].astype(F32)
    for k in range(3):
        a = a + yrecv[k].astype(F32)
    ys[...] = a.astype(BF)
    ng = [
        send(ys.at[pl.ds(up4(j, 1) * 4, 4)], nrecv.at[0], zp1),
        send(ys.at[pl.ds(up4(j, 3) * 4, 4)], nrecv.at[1], zm1),
        send(ys.at[pl.ds(up4(j, 2) * 4, 2)], n2recv.at[pl.ds(0, 2)], zp2),
        send(ys.at[pl.ds(up4(j, 2) * 4 + 2, 2)], n2recv.at[pl.ds(2, 2)], zm2),
    ]
    gr_ref[h] = xsum(1, h)
    for cp in ng:
        cp.wait_recv()
    a = ys[pl.ds(j * 4, 4)].astype(F32) + nrecv[0].astype(F32)
    a = a + nrecv[1].astype(F32) + n2recv[...].astype(F32)
    fs[:, 0:GROWS, :] = a.reshape(8, GROWS, 128).astype(BF)

    def own(k):
        return lax.rem(q + k + 8, 8)

    fa = send(fs.at[own(4)], rp.at[0], zp4)
    fb = send(fs.at[own(-3)], rm.at[0], zm4)

    def back(step):
        for i, (d, s, r) in enumerate(parts):
            zw[i].wait_recv()
            rows = pl.ds(r, 16)
            dst = pz.at[step, rows] if step < 3 else pz.at[3, rows]
            zw[i] = send(pz.at[step - 1, rows], dst, d)

    for step in (1, 2, 3):
        fa.wait_recv()
        sp[step - 1] = (rp[step - 1].astype(F32) + fs[own(4 - step)].astype(F32)).astype(BF)
        fa = send(sp.at[step - 1], rp.at[step], zp4)
        fb.wait_recv()
        if step < 3:
            sm[step - 1] = (rm[step - 1].astype(F32) + fs[own(step - 3)].astype(F32)).astype(BF)
            fb = send(sm.at[step - 1], rm.at[step], zm4)
        back(step)
    fa.wait_recv()
    ig_ref[...] = (fs[q].astype(F32) + rm[2].astype(F32) + rp[3].astype(F32)).astype(BF)
    for cp in zw:
        cp.wait_recv()
    gr_ref[1 - h] = pz[3]
    for cp in started:
        cp.wait_send()


def local(tokens, cotangent, gate_weight, up_weight, down_weight):
    xp = jnp.concatenate([tokens, cotangent], axis=0)
    xp = xp.reshape(4, 16, 2, HALF).transpose(0, 2, 1, 3).reshape(SHARD, 128)
    down = down_weight.T
    pad = jnp.zeros((2 * HALF, PACK - 3 * UNITS), BF)
    halves = []
    for i in range(2):
        cut = slice(i * UNITS, (i + 1) * UNITS)
        w = jnp.concatenate([gate_weight[:, cut], up_weight[:, cut], down[:, cut], pad], axis=1)
        halves.append(jnp.concatenate([w[:HALF], w[HALF:]], axis=1))
    wp = jnp.stack(halves)
    vmem = pl.BlockSpec(memory_space=pltpu.VMEM)
    ig, gr = pl.pallas_call(
        kernel,
        name="swiglu_backward",
        out_shape=(
            jax.ShapeDtypeStruct((GPAD, 128), BF),
            jax.ShapeDtypeStruct((2, HALF, WIDTH), BF),
        ),
        in_specs=[vmem, vmem],
        out_specs=(vmem, vmem),
        scratch_shapes=[
            pltpu.VMEM((128, SHARD, 128), BF),
            pltpu.VMEM((32 * SHARD, 128), F32),
            pltpu.VMEM((512, 2560), BF),
            pltpu.VMEM((16, HALF, WIDTH), BF),
            pltpu.VMEM((3, HALF, WIDTH), BF),
            pltpu.VMEM((512, WIDTH), F32),
            pltpu.VMEM((512, WIDTH), BF),
            pltpu.VMEM((512, WIDTH), BF),
            pltpu.VMEM((128 * GROWS, 128), F32),
            pltpu.VMEM((64, 80, 128), BF),
            pltpu.VMEM((16, HALF, WIDTH), BF),
            pltpu.VMEM((8, HALF, WIDTH), BF),
            pltpu.VMEM((8, HALF, WIDTH), BF),
            pltpu.VMEM((2, 3, HALF, WIDTH), BF),
            pltpu.VMEM((HALF, WIDTH), BF),
            pltpu.VMEM((4, HALF, WIDTH), BF),
            pltpu.VMEM((3, 16, 80, 128), BF),
            pltpu.VMEM((16, 80, 128), BF),
            pltpu.VMEM((2, 4, 80, 128), BF),
            pltpu.VMEM((4, 80, 128), BF),
            pltpu.VMEM((8, GPAD, 128), BF),
            pltpu.VMEM((4, GPAD, 128), BF),
            pltpu.VMEM((3, GPAD, 128), BF),
            pltpu.VMEM((3, GPAD, 128), BF),
            pltpu.VMEM((2, GPAD, 128), BF),
            pltpu.SemaphoreType.DMA((COPIES,)),
            pltpu.SemaphoreType.DMA((COPIES,)),
        ],
        compiler_params=pltpu.CompilerParams(
            collective_id=0, has_side_effects=True, vmem_limit_bytes=50 * 1024 * 1024
        ),
    )(xp, wp)
    input_grad = ig[:GROWS].reshape(2, 2, 16, HALF).transpose(0, 2, 1, 3).reshape(2, 2560)
    blocks = [jnp.concatenate([gr[i, :, :PACK], gr[i, :, PACK:]], axis=0) for i in range(2)]
    gate, up, down = (
        jnp.concatenate([b[:, i * UNITS : (i + 1) * UNITS] for b in blocks], axis=1)
        for i in range(3)
    )
    return input_grad, gate, up, down.T


def solution(mesh):
    placed = (
        P(("dp", "tensor"), None),
        P(("dp", "tensor"), None),
        P("dp", "tensor"),
        P("dp", "tensor"),
        P("tensor", "dp"),
    )
    return jax.shard_map(
        local,
        mesh=mesh,
        in_specs=placed,
        out_specs=(
            P(("dp", "tensor"), None),
            P("dp", "tensor"),
            P("dp", "tensor"),
            P("tensor", "dp"),
        ),
        check_vma=False,
    )
```

time: 1920 us -> 144 us (0.07)
  the two profiles are of different devices: /device:TPU:6 before, /device:TPU:102 now
where the time goes in v2:
time: 144 us; the launch traced here: 143 us
  Pallas kernels  136 us (94%)
  local copies, waits for them, and re-layouts  3.93 us (3%)
  other arithmetic  2.76 us (2%)
    pallas_call x1, Pallas kernels, local(): pl.pallas_call(kernel, name='swiglu_backward', out_shape=(jax.ShapeDtypeS...  136 us

profile of v2, /device:TPU:102, one launch (start us, length us, event | category | flops | bytes accessed | tf_op | source)
XLA Modules:
  0.0 143.4 jit_solution(15196708902700511909)
XLA Ops:
  0.6 0.0 copy-start
  0.6 1.1 fusion.14
  1.7 0.0 copy-done
  1.7 0.0 copy-start.1
  1.7 0.1 fusion.15
  1.8 0.8 copy-done.1
  2.6 0.1 fusion.16
  2.7 0.1 pad.23.clone
  2.8 0.2 maximum_maximum_fusion
  3.0 0.1 maximum_bitcast_fusion
  3.1 0.1 maximum_bitcast_fusion.1
  3.1 0.0 copy-start.2
  3.2 0.0 copy-start.3
  3.2 0.6 copy-done.2
  3.9 0.0 copy-done.3
  3.9 0.1 reshape.20
  4.0 0.1 reshape.21.xp_ref
  4.1 136.0 %swiglu_backward.1 = (bf16[48,128]{1,0:T(8,128)(2,1)S(1)}, bf16[2,80,640]{2,1,0:T(8,128)(2,1)S(1)}) custom-call(bf16[80,128]{1,0:T(8,128)(2,1)S(1)} %reshape.21.xp_ref, bf16[2,80,640]{2,1,0:T(8,128)(2,1)S(1)} %pad_maximum_fusion.wp_ref), custom_call_target="tpu_custom_call" | custom-call | tf_op jit(solution)/shard_map/swiglu_backward/pallas_call | solution.py:295
  140.1 0.1 slice_bitcast_fusion.2
  140.2 0.7 fusion.6
  141.0 0.1 fusion.10
  141.1 0.1 fusion.8
  141.2 0.7 pad_maximum_fusion.2
  141.9 0.7 pad_maximum_fusion.1
  142.6 0.1 reshape.22
  142.7 0.7 reshape.23
  (7 shorter events, 0.1 us)
Async XLA Ops:
  0.6 1.1 copy-start
  1.7 0.9 copy-start.1
  3.1 0.7 copy-start.2
  3.2 0.7 copy-start.3

commit v3 on v2

v3 whole, which is shorter than its diff:
```python
import jax
import jax.numpy as jnp
from jax import lax
from jax.experimental import pallas as pl
from jax.experimental.pallas import tpu as pltpu
from jax.sharding import PartitionSpec as P

MESH = pl.DeviceIdType.MESH
BF = jnp.bfloat16
F32 = jnp.float32
SHARD = 80
GROWS = 40
GPAD = 48
UNITS = 100
PACK = 320
WIDTH = 2 * PACK
HALF = 80
COPIES = 192


FIRST = [0, 5, 13, 21, 29]
COUNT = [5, 8, 8, 8, 3]
RING = [0, 1, 3, 5, 7]


def kernel(
    xp_ref, wp_ref, ig_ref, gr_ref,
    tokb, xf, xs, wbuf, wz, fwd, ab1, ab2, of, ob, pbuf, crecv, psum, xrecv, zsum, pz,
    yrecv, ys, na, n2, rp, rm, sp, sm, ssem, rsem,
):
    dp = lax.axis_index("dp")
    t = lax.axis_index("tensor")
    x, h, c = dp // 4, (dp // 2) % 2, dp % 2
    zl, y = t // 4, t % 4
    z = h * 16 + zl

    def dev(x=x, z=z, c=c, y=y):
        z = lax.rem(z + 32, 32)
        return ((x * 2 + z // 16) * 2 + c, lax.rem(z, 16) * 4 + y)

    def up4(v, k):
        return lax.rem(v + k, 4)

    zp4, zm4, zp1, zm1, zp2, zm2 = [dev(z=z + k) for k in (4, -4, 1, -1, 2, -2)]
    yp1, yp2, ym1 = [dev(y=up4(y, k)) for k in (1, 2, 3)]
    xpeer = [dev(x=up4(x, k)) for k in (1, 2, 3)]
    sib = dev(c=1 - c)
    partners = [zp4, zm4, zp1, zm1, zp2, zm2, yp1, yp2, ym1] + xpeer + [sib]
    turn = 4 - 8 * c
    ahead, behind = dev(z=z + turn), dev(z=z - turn)
    parts = [(ahead, turn, 0), (ahead, turn, 16), (ahead, turn, 32), (behind, -turn, 48), (behind, -turn, 64)]

    counter = [0]
    started = []

    def send(src, dst, device):
        i = counter[0]
        counter[0] += 1
        cp = pltpu.make_async_remote_copy(
            src_ref=src, dst_ref=dst, send_sem=ssem.at[i], recv_sem=rsem.at[i],
            device_id=device, device_id_type=MESH,
        )
        cp.start()
        started.append(cp)
        return cp

    def arrive(cps):
        for cp in cps:
            cp.wait_recv()

    barrier = pltpu.get_barrier_semaphore()
    for d in partners:
        pl.semaphore_signal(barrier, inc=1, device_id=d, device_id_type=MESH)
    tokb[0] = xp_ref[...]
    wbuf[dp] = wp_ref[h]
    of[...] = jnp.zeros_like(of)
    pl.semaphore_wait(barrier, len(partners))

    def far(step):
        f = FIRST[step]
        to = FIRST[step + 1]
        if step == 0:
            return [send(tokb.at[0], tokb.at[to], zm4), send(tokb.at[0], tokb.at[to + 1], zp4)]
        if step < 3:
            return [send(tokb.at[f], tokb.at[to], zm4), send(tokb.at[f + 1], tokb.at[to + 1], zp4)]
        one, two = pl.ds(0, 48), pl.ds(48, 32)
        return [
            send(tokb.at[f, one], tokb.at[to, one], zm4),
            send(tokb.at[f + 1, two], tokb.at[to, two], zp4),
        ]

    def near(step):
        f = FIRST[step]
        if step in (0, 4):
            out = [send(tokb.at[f], tokb.at[f + 2], zp1), send(tokb.at[f], tokb.at[f + 1], zm1)]
            if step == 0:
                out += [send(tokb.at[0], tokb.at[3], zm2), send(tokb.at[0], tokb.at[4], zp2)]
            return out
        pair = tokb.at[pl.ds(f, 2)]
        return [
            send(pair, tokb.at[pl.ds(f + 4, 2)], zp1),
            send(pair, tokb.at[pl.ds(f + 2, 2)], zm1),
            send(tokb.at[f], tokb.at[f + 6], zm2),
            send(tokb.at[f + 1], tokb.at[f + 7], zp2),
        ]

    def yfirst(step):
        src = tokb.at[pl.ds(FIRST[step], COUNT[step])]
        return [
            send(src, tokb.at[pl.ds(32 + FIRST[step], COUNT[step])], yp1),
            send(src, tokb.at[pl.ds(64 + FIRST[step], COUNT[step])], ym1),
        ]

    def ysecond(step, cps):
        f, n = FIRST[step], COUNT[step]
        k = n // 2
        cps[0].wait_recv()
        out = [send(tokb.at[pl.ds(32 + f, k)], tokb.at[pl.ds(96 + f, k)], yp1)]
        cps[1].wait_recv()
        out.append(send(tokb.at[pl.ds(64 + f + k, n - k)], tokb.at[pl.ds(96 + f + k, n - k)], ym1))
        return out

    zw = []

    def relay(step):
        for i, (d, s, r) in enumerate(parts):
            rows = pl.ds(r, 16)
            if step == 0:
                zw.append(send(wp_ref.at[1 - h, rows], wz.at[0, rows], d))
                continue
            zw[i].wait_recv()
            if step < 3:
                dst = wz.at[step, rows]
            else:
                to = lax.rem(z + s + 32, 32) // 16
                dst = wbuf.at[(x * 2 + 1 - to) * 2 + c, rows]
            zw[i] = send(wz.at[step - 1, rows], dst, d)

    fc = [far(0)]
    nc = [near(0)]
    relay(0)
    xown = [send(wbuf.at[dp], wbuf.at[dp], xpeer[k]) for k in range(3)]
    core_c = [send(wbuf.at[dp], wbuf.at[dp], sib)]
    y1, y2 = [], []
    for step in (1, 2, 3, 4):
        arrive(fc[step - 1])
        if step < 4:
            fc.append(far(step))
        nc.append(near(step))
        arrive(nc[step - 1])
        y1.append(yfirst(step - 1))
        if step < 4:
            relay(step)
        if step == 1:
            for k in range(3):
                xown[k].wait_recv()
                s = (up4(x, 3 - k) * 2 + h) * 2 + c
                core_c.append(send(wbuf.at[s], wbuf.at[s], sib))
        else:
            y2.append(ysecond(step - 2, y1[step - 2]))
    arrive(nc[4])
    y1.append(yfirst(4))
    other = (x * 2 + 1 - h) * 2 + c
    groups = [(pl.ds(0, 48), zw[:3]), (pl.ds(48, 32), zw[3:])]
    xfw = []
    for rows, cps in groups:
        arrive(cps)
        block = wbuf.at[other, rows]
        xfw.append([send(block, block, xpeer[k]) for k in range(3)])
        core_c.append(send(block, block, sib))
    y2.append(ysecond(3, y1[3]))

    def unpack(yy):
        xf[...] = tokb[yy * 32 : yy * 32 + 32].astype(F32).reshape(32 * SHARD, 128)
        for a in range(2):
            for k in range(2):
                row = a * 256 + yy * 64 + k * 32
                for b in range(20):
                    v = xf[pl.ds(a * 40 + k * 20 + b, 32, stride=SHARD), :]
                    xs[row : row + 32, b * 128 : b * 128 + 128] = v.astype(BF)

    y2.append(ysecond(4, y1[4]))
    for i, (rows, cps) in enumerate(groups):
        for k in range(3):
            cps = xfw[i][k]
            cps.wait_recv()
            block = wbuf.at[(up4(x, 3 - k) * 2 + 1 - h) * 2 + c, rows]
            core_c.append(send(block, block, sib))
    unpack(0)
    unpack(1)
    unpack(2)
    for cps in y2:
        arrive(cps)
    unpack(3)
    arrive(core_c)

    w = wbuf[...].reshape(1280, WIDTH)
    fwd[...] = jnp.dot(xs[:, 1280:2560], w, preferred_element_type=F32)
    fwd[...] = jnp.dot(xs[:, 0:1280], w, preferred_element_type=F32) + pltpu.roll(
        fwd[...], PACK, 1
    )
    g = fwd[0:256, :256]
    gate = g[:, :128]
    upv = pltpu.roll(g, 256 - UNITS, 1)[:, :128]
    hg = pltpu.roll(fwd[256:512, :384], 384 - 2 * UNITS, 1)[:, :128]
    sig = 1.0 / (1.0 + jnp.exp(-gate))
    keep = lax.broadcasted_iota(jnp.int32, (256, 128), 1) < UNITS
    rest = jnp.zeros((256, WIDTH - 128), F32)

    def wide(v):
        return jnp.concatenate([jnp.where(keep, v, 0.0), rest], axis=1)

    gg = wide(hg * upv * sig * (1.0 + gate * (1.0 - sig)))
    a = gg + pltpu.roll(wide(hg * gate * sig), UNITS, 1)
    ab1[0:256, :] = a.astype(BF)
    ab2[0:256, :] = pltpu.roll(a, PACK, 1).astype(BF)
    a = wide(gate * sig * upv)
    ab1[256:512, :] = pltpu.roll(a, 2 * UNITS, 1).astype(BF)
    ab2[256:512, :] = pltpu.roll(a, PACK + 2 * UNITS, 1).astype(BF)

    tr = (((0,), (0,)), ((), ()))
    for i in range(2):
        p = lax.dot_general(
            xs[:, i * 640 : i * 640 + 640], ab1[...], tr, preferred_element_type=F32
        ) + lax.dot_general(
            xs[:, 1280 + i * 640 : 1920 + i * 640], ab2[...], tr, preferred_element_type=F32
        )
        p = p.astype(BF)
        for b in range(8):
            pbuf[(b % 2) * 8 + ((b // 2) % 2) * 4 + i * 2 + b // 4] = p[b * HALF : (b + 1) * HALF, :]

    def core(hh):
        src = pl.ds((1 - c) * 8 + hh * 4, 4)
        return send(pbuf.at[src], crecv.at[pl.ds(hh * 4, 4)], sib)

    pc = core(1 - h)

    nt = (((1,), (1,)), ((), ()))
    for e, ab in enumerate((ab1, ab2)):
        for i in range(2):
            w = wbuf[i * 8 : i * 8 + 8].reshape(640, WIDTH)
            tot = lax.dot_general(ab[0:256, :], w, nt, preferred_element_type=F32)
            for yy in range(4):
                for k in range(2):
                    row = yy * 64 + k * 32
                    for b in range(5):
                        at = yy * 32 * GPAD + k * 20 + e * 10 + i * 5 + b
                        of[pl.ds(at, 32, stride=GPAD), :] = tot[row : row + 32, b * 128 : b * 128 + 128]
    ob[...] = of[...].reshape(128, GPAD, 128).astype(BF)

    yg = [None] * 5
    for step in (4, 3, 2, 1, 0):
        f, n = FIRST[step], COUNT[step]
        yg[step] = [
            send(ob.at[pl.ds(32 * (k + 1) + f, n)], yrecv.at[k, pl.ds(f, n)], d)
            for k, d in ((2, yp2), (0, ym1), (1, yp1))
        ]

    def ynear(step):
        f, n, r = FIRST[step], COUNT[step], RING[step]
        arrive(yg[step])
        a = ob[f : f + n].astype(F32)
        for k in range(3):
            a = a + yrecv[k, f : f + n].astype(F32)
        ys[f : f + n] = a.astype(BF)
        if step in (0, 4):
            out = [send(ys.at[f + 1], na.at[1, r], zp1), send(ys.at[f + 2], na.at[0, r], zm1)]
            if step == 0:
                out += [send(ys.at[3], n2.at[0, 0], zp2), send(ys.at[4], n2.at[1, 0], zm2)]
            return out
        return [
            send(ys.at[pl.ds(f + 2, 2)], na.at[1, pl.ds(r, 2)], zp1),
            send(ys.at[pl.ds(f + 4, 2)], na.at[0, pl.ds(r, 2)], zm1),
            send(ys.at[f + 6], n2.at[0, step], zp2),
            send(ys.at[f + 7], n2.at[1, step], zm2),
        ]

    def ringsum(step, k):
        f, r = FIRST[step] + k, RING[step] + k
        a = ys[f].astype(F32) + na[0, r].astype(F32) + na[1, r].astype(F32)
        if step < 4:
            a = a + n2[k, step].astype(F32)
        if step == 0:
            a = a + n2[1, 0].astype(F32)
        return a

    def coresum(hh):
        for i in range(4):
            a = pbuf[c * 8 + hh * 4 + i].astype(F32) + crecv[hh * 4 + i].astype(F32)
            psum[hh * 4 + i] = a.astype(BF)

    def xsend(n, hh):
        return [send(psum.at[hh * 4 + up4(x, k + 1)], xrecv.at[n, k], xpeer[k]) for k in range(3)]

    def xsum(n, hh, cps):
        arrive(cps)
        a = psum[hh * 4 + x].astype(F32)
        for k in range(3):
            a = a + xrecv[n, k].astype(F32)
        return (a * (1.0 / 16.0)).astype(BF)

    def back(step):
        for i, (d, s, r) in enumerate(parts):
            rows = pl.ds(r, 16)
            if step == 0:
                zw[i] = send(zsum.at[rows], pz.at[0, rows], d)
            else:
                zw[i].wait_recv()
                zw[i] = send(pz.at[step - 1, rows], pz.at[step, rows], d)

    def ringstep(step, plus, minus):
        arrive(ngc[step])
        if step == 4:
            sp[3] = ringsum(4, 0).astype(BF)
            return send(sp.at[3], rp.at[3], zp4), None
        plus.wait_recv()
        sp[step - 1] = (rp[step].astype(F32) + ringsum(step, 0)).astype(BF)
        plus = send(sp.at[step - 1], rp.at[step - 1], zp4)
        a = ringsum(step, 1)
        if step < 3:
            minus.wait_recv()
            a = a + rm[step].astype(F32)
        sm[step - 1] = a.astype(BF)
        minus = send(sm.at[step - 1], rm.at[step - 1], zm4)
        return plus, minus

    ngc = [None] * 5
    pc.wait_recv()
    pc = core(h)
    coresum(1 - h)
    px0 = xsend(0, 1 - h)
    ngc[4] = ynear(4)
    ngc[3] = ynear(3)
    plus, minus = ringstep(4, None, None)
    zsum[...] = xsum(0, 1 - h, px0)
    back(0)
    pc.wait_recv()
    coresum(h)
    px1 = xsend(1, h)
    ngc[2] = ynear(2)
    plus, minus = ringstep(3, plus, minus)
    ngc[1] = ynear(1)
    back(1)
    plus, minus = ringstep(2, plus, minus)
    ngc[0] = ynear(0)
    back(2)
    gr_ref[h] = xsum(1, h, px1)
    plus, minus = ringstep(1, plus, minus)
    back(3)
    arrive(ngc[0])
    plus.wait_recv()
    minus.wait_recv()
    ig_ref[...] = (ringsum(0, 0) + rp[0].astype(F32) + rm[0].astype(F32)).astype(BF)
    arrive(zw)
    gr_ref[1 - h] = pz[3]
    for cp in started:
        cp.wait_send()


def local(tokens, cotangent, gate_weight, up_weight, down_weight):
    xp = jnp.concatenate([tokens, cotangent], axis=0)
    xp = xp.reshape(4, 16, 2, HALF).transpose(0, 2, 1, 3).reshape(SHARD, 128)
    down = down_weight.T
    pad = jnp.zeros((2 * HALF, PACK - 3 * UNITS), BF)
    halves = []
    for i in range(2):
        cut = slice(i * UNITS, (i + 1) * UNITS)
        w = jnp.concatenate([gate_weight[:, cut], up_weight[:, cut], down[:, cut], pad], axis=1)
        halves.append(jnp.concatenate([w[:HALF], w[HALF:]], axis=1))
    wp = jnp.stack(halves)
    vmem = pl.BlockSpec(memory_space=pltpu.VMEM)
    ig, gr = pl.pallas_call(
        kernel,
        name="swiglu_backward",
        out_shape=(
            jax.ShapeDtypeStruct((GPAD, 128), BF),
            jax.ShapeDtypeStruct((2, HALF, WIDTH), BF),
        ),
        in_specs=[vmem, vmem],
        out_specs=(vmem, vmem),
        scratch_shapes=[
            pltpu.VMEM((128, SHARD, 128), BF),
            pltpu.VMEM((32 * SHARD, 128), F32),
            pltpu.VMEM((512, 2560), BF),
            pltpu.VMEM((16, HALF, WIDTH), BF),
            pltpu.VMEM((3, HALF, WIDTH), BF),
            pltpu.VMEM((512, WIDTH), F32),
            pltpu.VMEM((512, WIDTH), BF),
            pltpu.VMEM((512, WIDTH), BF),
            pltpu.VMEM((128 * GPAD, 128), F32),
            pltpu.VMEM((128, GPAD, 128), BF),
            pltpu.VMEM((16, HALF, WIDTH), BF),
            pltpu.VMEM((8, HALF, WIDTH), BF),
            pltpu.VMEM((8, HALF, WIDTH), BF),
            pltpu.VMEM((2, 3, HALF, WIDTH), BF),
            pltpu.VMEM((HALF, WIDTH), BF),
            pltpu.VMEM((4, HALF, WIDTH), BF),
            pltpu.VMEM((3, 32, GPAD, 128), BF),
            pltpu.VMEM((32, GPAD, 128), BF),
            pltpu.VMEM((2, 8, GPAD, 128), BF),
            pltpu.VMEM((2, 4, GPAD, 128), BF),
            pltpu.VMEM((4, GPAD, 128), BF),
            pltpu.VMEM((3, GPAD, 128), BF),
            pltpu.VMEM((4, GPAD, 128), BF),
            pltpu.VMEM((3, GPAD, 128), BF),
            pltpu.SemaphoreType.DMA((COPIES,)),
            pltpu.SemaphoreType.DMA((COPIES,)),
        ],
        compiler_params=pltpu.CompilerParams(
            collective_id=0, has_side_effects=True, vmem_limit_bytes=50 * 1024 * 1024
        ),
    )(xp, wp)
    input_grad = ig[:GROWS].reshape(2, 2, 16, HALF).transpose(0, 2, 1, 3).reshape(2, 2560)
    blocks = [jnp.concatenate([gr[i, :, :PACK], gr[i, :, PACK:]], axis=0) for i in range(2)]
    gate, up, down = (
        jnp.concatenate([b[:, i * UNITS : (i + 1) * UNITS] for b in blocks], axis=1)
        for i in range(3)
    )
    return input_grad, gate, up, down.T


def solution(mesh):
    placed = (
        P(("dp", "tensor"), None),
        P(("dp", "tensor"), None),
        P("dp", "tensor"),
        P("dp", "tensor"),
        P("tensor", "dp"),
    )
    return jax.shard_map(
        local,
        mesh=mesh,
        in_specs=placed,
        out_specs=(
            P(("dp", "tensor"), None),
            P("dp", "tensor"),
            P("dp", "tensor"),
            P("tensor", "dp"),
        ),
        check_vma=False,
    )
```

time: 144 us -> 121 us (0.84)
  the two profiles are of different devices: /device:TPU:102 before, /device:TPU:6 now
where the time goes in v3:
time: 121 us; the launch traced here: 120 us
  Pallas kernels  113 us (93%)
  local copies, waits for them, and re-layouts  3.93 us (3%)
  other arithmetic  2.76 us (2%)
    pallas_call x1, Pallas kernels, local(): pl.pallas_call(kernel, name='swiglu_backward', out_shape=(jax.ShapeDtypeS...  113 us

profile of v3, /device:TPU:6, one launch (start us, length us, event | category | flops | bytes accessed | tf_op | source)
XLA Modules:
  0.0 120.3 jit_solution(16388738191738515651)
XLA Ops:
  0.6 0.0 copy-start
  0.6 1.1 fusion.14
  1.7 0.0 copy-done
  1.7 0.0 copy-start.1
  1.7 0.1 fusion.15
  1.8 0.8 copy-done.1
  2.6 0.1 fusion.16
  2.7 0.1 pad.23.clone
  2.8 0.2 maximum_maximum_fusion
  3.0 0.1 maximum_bitcast_fusion
  3.1 0.1 maximum_bitcast_fusion.1
  3.1 0.0 copy-start.2
  3.2 0.0 copy-start.3
  3.2 0.6 copy-done.2
  3.9 0.0 copy-done.3
  3.9 0.1 reshape.20
  4.0 0.1 reshape.21.xp_ref
  4.1 112.9 %swiglu_backward.1 = (bf16[48,128]{1,0:T(8,128)(2,1)S(1)}, bf16[2,80,640]{2,1,0:T(8,128)(2,1)S(1)}) custom-call(bf16[80,128]{1,0:T(8,128)(2,1)S(1)} %reshape.21.xp_ref, bf16[2,80,640]{2,1,0:T(8,128)(2,1)S(1)} %pad_maximum_fusion.wp_ref), custom_call_target="tpu_custom_call" | custom-call | tf_op jit(solution)/shard_map/swiglu_backward/pallas_call | solution.py:372
  117.0 0.1 slice_bitcast_fusion.2
  117.1 0.7 fusion.6
  117.9 0.1 fusion.10
  118.0 0.1 fusion.8
  118.1 0.7 pad_maximum_fusion.2
  118.8 0.7 pad_maximum_fusion.1
  119.5 0.1 reshape.22
  119.6 0.7 reshape.23
  (7 shorter events, 0.1 us)
Async XLA Ops:
  0.6 1.1 copy-start
  1.7 0.9 copy-start.1
  3.1 0.7 copy-start.2
  3.2 0.7 copy-start.3

commit v4 on v3

--- a/solution.py
+++ b/solution.py
@@ -218,23 +218,6 @@
     ab1[256:512, :] = pltpu.roll(a, 2 * UNITS, 1).astype(BF)
     ab2[256:512, :] = pltpu.roll(a, PACK + 2 * UNITS, 1).astype(BF)
 
-    tr = (((0,), (0,)), ((), ()))
-    for i in range(2):
-        p = lax.dot_general(
-            xs[:, i * 640 : i * 640 + 640], ab1[...], tr, preferred_element_type=F32
-        ) + lax.dot_general(
-            xs[:, 1280 + i * 640 : 1920 + i * 640], ab2[...], tr, preferred_element_type=F32
-        )
-        p = p.astype(BF)
-        for b in range(8):
-            pbuf[(b % 2) * 8 + ((b // 2) % 2) * 4 + i * 2 + b // 4] = p[b * HALF : (b + 1) * HALF, :]
-
-    def core(hh):
-        src = pl.ds((1 - c) * 8 + hh * 4, 4)
-        return send(pbuf.at[src], crecv.at[pl.ds(hh * 4, 4)], sib)
-
-    pc = core(1 - h)
-
     nt = (((1,), (1,)), ((), ()))
     for e, ab in enumerate((ab1, ab2)):
         for i in range(2):
@@ -255,6 +238,23 @@
             send(ob.at[pl.ds(32 * (k + 1) + f, n)], yrecv.at[k, pl.ds(f, n)], d)
             for k, d in ((2, yp2), (0, ym1), (1, yp1))
         ]
+
+    tr = (((0,), (0,)), ((), ()))
+    for i in range(2):
+        p = lax.dot_general(
+            xs[:, i * 640 : i * 640 + 640], ab1[...], tr, preferred_element_type=F32
+        ) + lax.dot_general(
+            xs[:, 1280 + i * 640 : 1920 + i * 640], ab2[...], tr, preferred_element_type=F32
+        )
+        p = p.astype(BF)
+        for b in range(8):
+            pbuf[(b % 2) * 8 + ((b // 2) % 2) * 4 + i * 2 + b // 4] = p[b * HALF : (b + 1) * HALF, :]
+
+    def core(hh):
+        src = pl.ds((1 - c) * 8 + hh * 4, 4)
+        return send(pbuf.at[src], crecv.at[pl.ds(hh * 4, 4)], sib)
+
+    pc = core(1 - h)
 
     def ynear(step):
         f, n, r = FIRST[step], COUNT[step], RING[step]

time: 121 us -> 119 us (0.983)
    pallas_call x1, Pallas kernels: 113 us -> 112 us  [local(): pl.pallas_call(kernel, name='swiglu_backward', out_shape=(jax.ShapeDtypeS...]
where the time goes in v4:
time: 119 us
  Pallas kernels  112 us (94%)
  local copies, waits for them, and re-layouts  3.93 us (3%)
  other arithmetic  2.76 us (2%)
    pallas_call x1, Pallas kernels, local(): pl.pallas_call(kernel, name='swiglu_backward', out_shape=(jax.ShapeDtypeS...  112 us

profile of v4, /device:TPU:6, one launch (start us, length us, event | category | flops | bytes accessed | tf_op | source)
XLA Modules:
  0.0 119.1 jit_solution(9569507883596779724)
XLA Ops:
  0.6 0.0 copy-start
  0.6 1.1 fusion.14
  1.7 0.0 copy-done
  1.7 0.0 copy-start.1
  1.7 0.1 fusion.15
  1.8 0.8 copy-done.1
  2.6 0.1 fusion.16
  2.7 0.1 pad.23.clone
  2.8 0.2 maximum_maximum_fusion
  3.0 0.1 maximum_bitcast_fusion
  3.1 0.1 maximum_bitcast_fusion.1
  3.1 0.0 copy-start.2
  3.2 0.0 copy-start.3
  3.2 0.6 copy-done.2
  3.9 0.0 copy-done.3
  3.9 0.1 reshape.20
  4.0 0.1 reshape.21.xp_ref
  4.1 111.6 %swiglu_backward.1 = (bf16[48,128]{1,0:T(8,128)(2,1)S(1)}, bf16[2,80,640]{2,1,0:T(8,128)(2,1)S(1)}) custom-call(bf16[80,128]{1,0:T(8,128)(2,1)S(1)} %reshape.21.xp_ref, bf16[2,80,640]{2,1,0:T(8,128)(2,1)S(1)} %pad_maximum_fusion.wp_ref), custom_call_target="tpu_custom_call" | custom-call | tf_op jit(solution)/shard_map/swiglu_backward/pallas_call | solution.py:372
  115.8 0.1 slice_bitcast_fusion.2
  115.9 0.7 fusion.6
  116.6 0.1 fusion.10
  116.7 0.1 fusion.8
  116.8 0.7 pad_maximum_fusion.2
  117.5 0.7 pad_maximum_fusion.1
  118.3 0.1 reshape.22
  118.4 0.7 reshape.23
  (7 shorter events, 0.1 us)
Async XLA Ops:
  0.6 1.1 copy-start
  1.7 0.9 copy-start.1
  3.1 0.7 copy-start.2
  3.2 0.7 copy-start.3
